TPU v7x, 32 devices: a whole 2x2x4 slice. The times are simulated.
32 devices in a mesh: batch: 2 (over x), seq: 8 (over z, y), mp: 2 (over core).
Axes of the slice: x: 2, y: 2, z: 4, core: 2. Of those that a mesh axis runs over, the one named last changes fastest.
Arguments:
- tokens: bfloat16 [8192, 2048], P(('batch', 'seq'), 'mp'), parts along dimension 0, may hold values from -36 to 36
- modulation: float32 [12, 2048], P('batch'), parts along dimension 0, may hold values from -3 to 3
- query_weight: bfloat16 [2048, 1024], P(None, 'mp'), may hold values from -0.125 to 0.125
- key_weight: bfloat16 [2048, 1024], P(None, 'mp'), may hold values from -0.125 to 0.125
- value_weight: bfloat16 [2048, 1024], P(None, 'mp'), may hold values from -0.125 to 0.125
- out_weight: bfloat16 [1024, 2048], P('mp'), may hold values from -0.1875 to 0.1875
- query_gain: float32 [128], replicated, may hold values from 1 to 2
- key_gain: float32 [128], replicated, may hold values from 1 to 2
- conv_weight: bfloat16 [27, 2048], P(None, 'mp'), may hold values from -1.25 to 1.25
Outputs:
- mixed: bfloat16 [8192, 2048], P(('batch', 'seq'), 'mp'), parts along dimension 0
There are 2 independent parts, one for each index of `batch`. A program takes and returns all parts, laid end to end along the dimension named above; an argument that names none is the same for every part. Nothing has to cross between parts.
All inputs are finite; a program needn't handle non-finite values.
Results may differ from a plain program's by a relative error of at most 0.0065.
Values may be sent and summed in bfloat16 or wider, within the bound.
A program may use at most 64 MiB of HBM per device.

v0:
```python
import jax
import jax.numpy as jnp
from jax import lax
from jax.sharding import PartitionSpec as P

D = 2048
HD = 128
GY = 8
GX = 16
REACH = 2
ZDEV = 4
PLANE = 128
RADIUS = 8


EPS = 1e-06


def passed_along(value, axis, steps):
    count = lax.axis_size(axis)
    pairs = [(source, (source + steps) % count) for source in range(count)]
    return lax.ppermute(value, axis, pairs)


def with_halo(array, sides, width):
    for axis, dim in sides:
        size, length = (lax.axis_size(axis), array.shape[dim])
        up = [(i, (i + 1) % size) for i in range(size)]
        down = [(j, i) for i, j in up]
        last = lax.slice_in_dim(array, length - width, length, axis=dim)
        initial = lax.slice_in_dim(array, 0, width, axis=dim)
        before = lax.ppermute(last, axis, up)
        after = lax.ppermute(initial, axis, down)
        array = jnp.concatenate([before, array, after], axis=dim)
    return array


def head_norm(values, gain_vec):
    mean_sq = jnp.mean(values * values, axis=-1, keepdims=True)
    return values * lax.rsqrt(mean_sq + EPS) * gain_vec


def on_device(
    tokens,
    modulation,
    query_weight,
    key_weight,
    value_weight,
    out_weight,
    query_gain,
    key_gain,
    conv_weight,
):
    tok_rows = tokens.shape[0]
    half_width = tokens.shape[1]
    heads_here = query_weight.shape[1] // HD
    offset = lax.axis_index("mp") * half_width
    local_mod = lax.dynamic_slice_in_dim(modulation, offset, half_width, 1)
    full_rows = lax.all_gather(tokens, "mp", axis=1, tiled=True)
    full_vals = full_rows.astype(jnp.float32)
    row_mean = jnp.mean(full_vals, axis=-1, keepdims=True)
    variance = jnp.mean(full_vals * full_vals, axis=-1, keepdims=True) - row_mean * row_mean
    normed = (
        (full_vals - row_mean) * lax.rsqrt(variance + EPS) * (1.0 + modulation[1]) + modulation[0]
    ).astype(jnp.bfloat16)
    queries = jnp.dot(normed, query_weight, preferred_element_type=jnp.float32).reshape(
        tok_rows, heads_here, HD
    )
    queries = (head_norm(queries, query_gain) * HD ** (-0.5)).astype(jnp.bfloat16)
    key_vals = jnp.dot(normed, key_weight, preferred_element_type=jnp.float32).reshape(
        tok_rows, heads_here, HD
    )
    key_vals = head_norm(key_vals, key_gain).astype(jnp.bfloat16).reshape(tok_rows, heads_here * HD)
    value_vals = jnp.dot(normed, value_weight, preferred_element_type=jnp.float32).astype(
        jnp.bfloat16
    )
    kv_pair = jnp.stack([key_vals, value_vals])
    plane_of = jnp.arange(tok_rows, dtype=jnp.int32) // PLANE

    def attend(state_pair, kv_block, shift_count):
        running, denom = state_pair
        key_blk = kv_block[0].reshape(tok_rows, heads_here, HD)
        value_blk = kv_block[1].reshape(tok_rows, heads_here, HD)
        scores = jnp.einsum("qhd,khd->hqk", queries, key_blk, preferred_element_type=jnp.float32)
        plane_gap = shift_count * ZDEV + plane_of[:, None] - plane_of[None, :]
        inside = jnp.abs(plane_gap) <= RADIUS
        weights = jnp.where(inside[None], jnp.exp(scores), jnp.float32(0.0))
        denom = denom + jnp.sum(weights, axis=-1)
        running = running + jnp.einsum(
            "hqk,khd->qhd",
            weights.astype(jnp.bfloat16),
            value_blk,
            preferred_element_type=jnp.float32,
        )
        return (running, denom)

    state_pair = (
        jnp.zeros((tok_rows, heads_here, HD), jnp.float32),
        jnp.zeros((heads_here, tok_rows), jnp.float32),
    )
    state_pair = attend(state_pair, kv_pair, 0)
    for shift_count in range(1, REACH + 1):
        from_below = passed_along(kv_pair, "seq", shift_count)
        state_pair = attend(state_pair, from_below, shift_count)
        from_above = passed_along(kv_pair, "seq", -shift_count)
        state_pair = attend(state_pair, from_above, -shift_count)
    running, denom = state_pair
    attn_out = (
        (running / jnp.transpose(denom)[:, :, None])
        .astype(jnp.bfloat16)
        .reshape(tok_rows, heads_here * HD)
    )
    partial_value = jnp.dot(attn_out, out_weight, preferred_element_type=jnp.float32)
    attended = lax.psum_scatter(
        partial_value.astype(jnp.bfloat16), "mp", scatter_dimension=1, tiled=True
    ).astype(jnp.float32)
    residual = tokens.astype(jnp.float32) + local_mod[2] * attended
    row_sum, sq_sum = lax.psum(
        (jnp.sum(residual, axis=-1), jnp.sum(residual * residual, axis=-1)), "mp"
    )
    center = (row_sum / D)[:, None]
    spread = (sq_sum / D)[:, None] - center * center
    shaped = (
        (residual - center) * lax.rsqrt(spread + EPS) * (1.0 + local_mod[4]) + local_mod[3]
    ).astype(jnp.bfloat16)
    grid_vals = shaped.reshape(ZDEV, GY, GX, half_width)
    padded = with_halo(grid_vals, (("seq", 0),), 1)
    padded = jnp.pad(padded, ((0, 0), (1, 1), (1, 1), (0, 0)))
    conv_taps = conv_weight.astype(jnp.float32)
    conv_sum = jnp.zeros((ZDEV, GY, GX, half_width), jnp.float32)
    for dz_off in range(3):
        for dy_off in range(3):
            for dx_off in range(3):
                window = padded[dz_off : dz_off + ZDEV, dy_off : dy_off + GY, dx_off : dx_off + GX]
                conv_sum = conv_sum + window * conv_taps[(dz_off * 3 + dy_off) * 3 + dx_off]
    mixed = residual + local_mod[5] * jax.nn.gelu(conv_sum.reshape(tok_rows, half_width))
    return mixed.astype(jnp.bfloat16)


def solution(mesh):
    return jax.shard_map(
        on_device,
        mesh=mesh,
        in_specs=(
            P(("batch", "seq"), "mp"),
            P("batch", None),
            P(None, "mp"),
            P(None, "mp"),
            P(None, "mp"),
            P("mp", None),
            P(),
            P(),
            P(None, "mp"),
        ),
        out_specs=P(("batch", "seq"), "mp"),
        check_vma=False,
    )
```

profile of v0, /device:TPU:0, one launch (start us, length us, event | category | flops | bytes accessed | tf_op | source)
XLA Modules:
  0.0 164.3 jit_solution(14295720424937571424)
XLA Ops:
  8.0 2.3 %abs_compare_fusion.3 = (pred[512,512]{0,1:T(8,128)(4,1)}, pred[512,512]{0,1:T(8,128)(4,1)}, pred[512,512]{0,1:T(8,128)(4,1)}, pred[512,512]{0,1:T(8,128)(4,1)}, pred[512,512]{0,1:T(8,128)(4,1)S(1)}) fusion(s32[512]{0:T(512)S(1)} %broadcast_add_fusion.3, s32[512]{0:T(512)S(1)} %get-tuple-element.77, s32[512]{0:T(512)S(1)} %get-tuple-element.79, ...), kind=kLoop, calls=%fused_computation.83 | loop fusion | flops 3932160 | bytes 1320960 | tf_op jit(solution)/shard_map/le | solution.py:86
  10.4 11.9 %all-gather.2.cloned.1.call-done = bf16[512,2048]{1,0:T(8,128)(2,1)} async-done(((bf16[512,1024]{1,0:T(8,128)(2,1)}), bf16[512,2048]{1,0:T(8,128)(2,1)}) %all-gather.2.cloned.1.call-update) | async-done | bytes 2097168 | tf_op jit(solution)/shard_map/all_gather | solution.py:59
  22.2 2.4 %convert_reduce_fusion = (f32[512]{0:T(512)S(1)}, f32[512]{0:T(512)S(1)}) fusion(bf16[512,2048]{1,0:T(8,128)(2,1)} %all-gather.2.cloned.1.call-done), kind=kLoop, calls=%fused_computation.6 | loop fusion | flops 4193280 | bytes 2101248 | tf_op jit(solution)/shard_map/reduce_sum | solution.py:61
  27.9 1.3 multiply_reduce_fusion.1
  30.5 3.6 %collective-permute-start.3 = (bf16[2,512,512]{1,2,0:T(8,128)(2,1)}, bf16[2,512,512]{1,2,0:T(8,128)(2,1)}, u32[]{:S(2)}, u32[]{:S(2)}) collective-permute-start(bf16[2,512,512]{1,2,0:T(8,128)(2,1)} %pad_maximum_fusion.2), channel_id=1, source_target_pairs={{0,12},{2,14},{4,0},{6,2},{8,4},{10,6},{12,8},{14,10},{1,13},{3,15... | collective-permute-start | bytes 3145736 | tf_op jit(solution)/shard_map/ppermute | solution.py:22
  34.1 4.7 %collective-permute-start.1 = (bf16[2,512,512]{1,2,0:T(8,128)(2,1)}, bf16[2,512,512]{1,2,0:T(8,128)(2,1)}, u32[]{:S(2)}, u32[]{:S(2)}) collective-permute-start(bf16[2,512,512]{1,2,0:T(8,128)(2,1)} %pad_maximum_fusion.2), channel_id=1, source_target_pairs={{0,14},{2,0},{4,2},{6,4},{8,6},{10,8},{12,10},{14,12},{1,15},{3,1}... | collective-permute-start | bytes 3145736 | tf_op jit(solution)/shard_map/ppermute | solution.py:22
  38.8 2.3 %multiply_reduce_fusion.2 = (f32[512,4]{0,1:T(4,128)S(1)}, f32[512,512]{0,1:T(8,128)}) fusion(bf16[512,2048]{1,0:T(8,128)(2,1)S(1)} %fusion.6, bf16[2048,512]{1,0:T(8,128)(2,1)S(1)} %copy-done.16), kind=kOutput, calls=%fused_computation.87 | convolution fusion | flops 1074264064 | bytes 5251072 | tf_op jit(solution)/shard_map/dot_general | solution.py:66
  41.2 2.5 %copy.10 = f32[512,4,128]{2,0,1:T(8,128)} copy(f32[512,4,128]{0,2,1:T(8,128)} %bitcast.104) | data formatting | bytes 2097152 | tf_op jit(solution)/shard_map/reshape | solution.py:66
  43.7 1.3 copy.11
  45.1 1.6 multiply_convert_fusion.1
  46.6 2.4 %fusion.8 = (f32[4,512]{1,0:T(4,128)S(1)}, f32[4,512,512]{1,2,0:T(8,128)S(1)}) fusion(pred[512,512]{0,1:T(8,128)(4,1)S(1)} %get-tuple-element.60, bf16[512,4,128]{2,0,1:T(8,128)(2,1)S(1)} %multiply_convert_fusion.1, f32[512,4,128]{2,0,1:T(8,128)} %copy.11, f32[128]{0:T(128)S(1)} %copy-done.12, f32[512,4]{0,1:T(4,128)S(1)} %add_rsqrt_fusion), kind=kOutput, calls=%fused_computation.20 | convolution fusion | flops 271316992 | bytes 6046208 | tf_op jit(solution)/shard_map/qhd,khd->hqk/dot_general | solution.py:84
  50.0 8.0 %collective-permute-done.3 = bf16[2,512,512]{1,2,0:T(8,128)(2,1)} collective-permute-done((bf16[2,512,512]{1,2,0:T(8,128)(2,1)}, bf16[2,512,512]{1,2,0:T(8,128)(2,1)}, u32[]{:S(2)}, u32[]{:S(2)}) %collective-permute-start.3) | collective-permute-done | bytes 1048608 | tf_op jit(solution)/shard_map/ppermute | solution.py:22
  60.4 21.1 %collective-permute-done.2 = bf16[2,512,512]{1,2,0:T(8,128)(2,1)} collective-permute-done((bf16[2,512,512]{1,2,0:T(8,128)(2,1)}, bf16[2,512,512]{1,2,0:T(8,128)(2,1)}, u32[]{:S(2)}, u32[]{:S(2)}) %collective-permute-start.2) | collective-permute-done | bytes 1048608 | tf_op jit(solution)/shard_map/ppermute | solution.py:22
  84.8 17.5 %collective-permute-done.1 = bf16[2,512,512]{1,2,0:T(8,128)(2,1)} collective-permute-done((bf16[2,512,512]{1,2,0:T(8,128)(2,1)}, bf16[2,512,512]{1,2,0:T(8,128)(2,1)}, u32[]{:S(2)}, u32[]{:S(2)}) %collective-permute-start.1) | collective-permute-done | bytes 1048608 | tf_op jit(solution)/shard_map/ppermute | solution.py:22
  110.2 2.9 %convolution_convert_fusion = bf16[512,2048]{1,0:T(8,128)(2,1)} fusion(bf16[512,512]{0,1:T(8,128)(2,1)S(1)} %bitcast.105, bf16[512,2048]{1,0:T(8,128)(2,1)S(1)} %copy-done), kind=kOutput, calls=%fused_computation.31 | convolution fusion | flops 1074790400 | bytes 4718592 | tf_op jit(solution)/shard_map/dot_general | solution.py:113
  113.2 11.5 %reduce-scatter.2.cloned.1.call-done = bf16[512,1024]{1,0:T(8,128)(2,1)} async-done(((bf16[512,2048]{1,0:T(8,128)(2,1)}), bf16[512,1024]{1,0:T(8,128)(2,1)}) %reduce-scatter.2.cloned.1.call-update) | async-done | bytes 1048592 | tf_op jit(solution)/shard_map/reduce_scatter | solution.py:114
  124.7 1.8 %fusion.66 = (f32[512]{0:T(512)S(1)}, f32[512]{0:T(512)S(1)}) fusion(bf16[512,1024]{1,0:T(8,128)(2,1)} %reduce-scatter.2.cloned.1.call-done, bf16[512,1024]{1,0:T(8,128)(2,1)S(1)} %copy-done.1, f32[1024]{0:T(1024)S(1)} %bitcast.108), kind=kLoop, calls=%fused_computation.71 | loop fusion | flops 3668992 | bytes 2105344 | tf_op jit(solution)/shard_map/reduce_sum | solution.py:119
  126.5 2.5 %all-reduce.1 = (f32[512]{0:T(512)S(1)}, f32[512]{0:T(512)S(1)}) all-reduce(f32[512]{0:T(512)S(1)} %get-tuple-element.6, f32[512]{0:T(512)S(1)} %get-tuple-element.5), channel_id=1, replica_groups=mesh['batch'=2,'seq'=8,'mp'=2] {'mp'}, use_global_device_ids=true, to_apply=%region_13.14 | all-reduce | flops 1024 | bytes 8192 | tf_op jit(solution)/shard_map/psum | solution.py:118
  129.0 1.8 %add_convert_fusion = bf16[512,1024]{1,0:T(8,128)(2,1)S(1)} fusion(bf16[512,1024]{1,0:T(8,128)(2,1)} %reduce-scatter.2.cloned.1.call-done, bf16[512,1024]{1,0:T(8,128)(2,1)S(1)} %copy-done.1, f32[1024]{0:T(1024)S(1)} %bitcast.142, f32[1024]{0:T(1024)S(1)} %bitcast.141, f32[512]{0:T(512)S(1)} %get-tuple-element.55, f32[512]{0:T(512)S(1)} %get-tuple-element.54, ...), kind=kLoop, calls=%fused_computation.53 | loop fusion | flops 4718592 | bytes 3162112 | tf_op jit(solution)/shard_map/convert_element_type | solution.py:125
  130.9 4.6 %collective-permute-start.5 = (bf16[1,8,16,1024]{3,2,1,0:T(8,128)(2,1)S(1)}, bf16[1,8,16,1024]{3,2,1,0:T(8,128)(2,1)S(1)}, u32[]{:S(2)}, u32[]{:S(2)}) collective-permute-start(bf16[1,8,16,1024]{3,2,1,0:T(8,128)(2,1)S(1)} %bitcast.107), channel_id=1, source_target_pairs={{2,0},{4,2},{6,4},{8,6},{10,8},{12,10},{14,12},{0,14},{3,1},{5,3},... | collective-permute-start | bytes 786440 | tf_op jit(solution)/shard_map/ppermute | solution.py:33
  135.6 5.9 %collective-permute-done.5 = bf16[1,8,16,1024]{3,2,1,0:T(8,128)(2,1)S(1)} collective-permute-done((bf16[1,8,16,1024]{3,2,1,0:T(8,128)(2,1)S(1)}, bf16[1,8,16,1024]{3,2,1,0:T(8,128)(2,1)S(1)}, u32[]{:S(2)}, u32[]{:S(2)}) %collective-permute-start.5) | collective-permute-done | bytes 262176 | tf_op jit(solution)/shard_map/ppermute | solution.py:33
  141.5 4.9 %collective-permute-done.4 = bf16[1,8,16,1024]{3,2,1,0:T(8,128)(2,1)S(1)} collective-permute-done((bf16[1,8,16,1024]{3,2,1,0:T(8,128)(2,1)S(1)}, bf16[1,8,16,1024]{3,2,1,0:T(8,128)(2,1)S(1)}, u32[]{:S(2)}, u32[]{:S(2)}) %collective-permute-start.4) | collective-permute-done | bytes 262176 | tf_op jit(solution)/shard_map/ppermute | solution.py:32
  147.5 7.9 %multiply_add_fusion = f32[4,8,16,1024]{3,2,1,0:T(8,128)S(1)} fusion(bf16[4,8,16,1024]{3,2,1,0:T(8,128)(2,1)S(1)} %bitcast.91, bf16[6,10,18,1024]{3,2,1,0:T(8,128)(2,1)S(1)} %select_maximum_fusion, bf16[1,8,16,1024]{3,2,1,0:T(8,128)(2,1)S(1)} %collective-permute-done.5, bf16[1,8,16,1024]{3,2,1,0:T(8,128)(2,1)S(1)} %collective-permute-done.4, ...), kind=kLoop, calls=%fused_computation.52 | loop fusion | flops 42991616 | bytes 28946432 | tf_op jit(solution)/shard_map/add | solution.py:135
  155.4 2.1 %fusion.30 = bf16[512,1024]{1,0:T(8,128)(2,1)} fusion(f32[4,8,16,1024]{3,2,1,0:T(8,128)S(1)} %multiply_add_fusion, bf16[512,1024]{1,0:T(8,128)(2,1)S(1)} %copy-done.2, bf16[512,1024]{1,0:T(8,128)(2,1)S(1)} %copy-done.1, f32[1024]{0:T(1024)S(1)} %bitcast.113, f32[1024]{0:T(1024)S(1)} %bitcast.110), kind=kLoop, calls=%fused_computation.46 | loop fusion | flops 7864320 | bytes 5251072 | tf_op jit(solution)/shard_map/convert_element_type | solution.py:137
  (74 shorter events, 21.8 us)
Async XLA Ops:
  6.5 103.7 %copy-start = (bf16[512,2048]{1,0:T(8,128)(2,1)S(1)}, bf16[512,2048]{1,0:T(8,128)(2,1)}, u32[]{:S(2)}) copy-start(bf16[512,2048]{1,0:T(8,128)(2,1)} %param.14) | copy-start | bytes 6291460
  6.5 3.8 %copy-start.11 = (f32[6,2048]{1,0:T(8,128)S(1)}, f32[6,2048]{1,0:T(8,128)}, u32[]{:S(2)}) copy-start(f32[6,2048]{1,0:T(8,128)} %param.10) | copy-start | bytes 147460
  6.5 15.7 %all-gather.2.cloned.1.call-start = ((), (), s32[]{:S(2)}) async-start(), calls=%async_computation.1 | async-start | bytes 3145728 | tf_op jit(solution)/shard_map/all_gather | solution.py:59
  7.3 117.5 %reduce-scatter.2.cloned.1.call-start = ((), (), s32[]{:S(2)}) async-start(), calls=%async_computation.2 | async-start | bytes 3145728 | tf_op jit(solution)/shard_map/reduce_scatter | solution.py:114
  22.2 2.5 %copy-start.3 = (bf16[512,2048]{1,0:T(8,128)(2,1)S(1)}, bf16[512,2048]{1,0:T(8,128)(2,1)}, u32[]{:S(2)}) copy-start(bf16[512,2048]{1,0:T(8,128)(2,1)} %all-gather.2.cloned.1.call-done) | copy-start | bytes 6291460
  24.7 1.6 copy-start.14
  26.3 1.6 copy-start.15
  27.9 1.6 copy-start.8
  29.2 9.6 %copy-start.16 = (bf16[2048,512]{1,0:T(8,128)(2,1)S(1)}, bf16[2048,512]{1,0:T(8,128)(2,1)}, u32[]{:S(2)}) copy-start(bf16[2048,512]{1,0:T(8,128)(2,1)} %param.11) | copy-start | bytes 6291460
  30.5 27.5 %collective-permute-start.3 = (bf16[2,512,512]{1,2,0:T(8,128)(2,1)}, bf16[2,512,512]{1,2,0:T(8,128)(2,1)}, u32[]{:S(2)}, u32[]{:S(2)}) collective-permute-start(bf16[2,512,512]{1,2,0:T(8,128)(2,1)} %pad_maximum_fusion.2), channel_id=1, source_target_pairs={{0,12},{2,14},{4,0},{6,2},{8,4},{10,6},{12,8},{14,10},{1,13},{3,15... | collective-permute-start | bytes 3145736 | tf_op jit(solution)/shard_map/ppermute | solution.py:22
  34.1 47.3 %collective-permute-start.2 = (bf16[2,512,512]{1,2,0:T(8,128)(2,1)}, bf16[2,512,512]{1,2,0:T(8,128)(2,1)}, u32[]{:S(2)}, u32[]{:S(2)}) collective-permute-start(bf16[2,512,512]{1,2,0:T(8,128)(2,1)} %pad_maximum_fusion.2), channel_id=1, source_target_pairs={{0,4},{2,6},{4,8},{6,10},{8,12},{10,14},{12,0},{14,2},{1,5},{3,7},... | collective-permute-start | bytes 3145736 | tf_op jit(solution)/shard_map/ppermute | solution.py:22
  34.1 68.2 %collective-permute-start.1 = (bf16[2,512,512]{1,2,0:T(8,128)(2,1)}, bf16[2,512,512]{1,2,0:T(8,128)(2,1)}, u32[]{:S(2)}, u32[]{:S(2)}) collective-permute-start(bf16[2,512,512]{1,2,0:T(8,128)(2,1)} %pad_maximum_fusion.2), channel_id=1, source_target_pairs={{0,14},{2,0},{4,2},{6,4},{8,6},{10,8},{12,10},{14,12},{1,15},{3,1}... | collective-permute-start | bytes 3145736 | tf_op jit(solution)/shard_map/ppermute | solution.py:22
  38.8 67.8 %collective-permute-start = (bf16[2,512,512]{1,2,0:T(8,128)(2,1)}, bf16[2,512,512]{1,2,0:T(8,128)(2,1)}, u32[]{:S(2)}, u32[]{:S(2)}) collective-permute-start(bf16[2,512,512]{1,2,0:T(8,128)(2,1)} %pad_maximum_fusion.2), channel_id=1, source_target_pairs={{0,2},{2,4},{4,6},{6,8},{8,10},{10,12},{12,14},{14,0},{1,3},{3,5},... | collective-permute-start | bytes 3145736 | tf_op jit(solution)/shard_map/ppermute | solution.py:22
  41.1 3.9 %copy-start.13 = (f32[128]{0:T(128)S(1)}, f32[128]{0:T(128)}, u32[]{:S(2)}) copy-start(f32[128]{0:T(128)} %param.15) | copy-start | bytes 1540
  43.7 2.9 %copy-start.12 = (f32[128]{0:T(128)S(1)}, f32[128]{0:T(128)}, u32[]{:S(2)}) copy-start(f32[128]{0:T(128)} %param.16) | copy-start | bytes 1540
  46.6 2.4 %copy-start.9 = (bf16[512,512]{0,1:T(8,128)(2,1)S(1)}, bf16[512,512]{0,1:T(8,128)(2,1)}, u32[]{:S(2)}) copy-start(bf16[512,512]{0,1:T(8,128)(2,1)} %copy-done.8) | copy-start | bytes 1572868
  50.0 9.2 %copy-start.7 = (pred[512,512]{0,1:T(8,128)(4,1)S(1)}, pred[512,512]{0,1:T(8,128)(4,1)}, u32[]{:S(2)}) copy-start(pred[512,512]{0,1:T(8,128)(4,1)} %get-tuple-element.58) | copy-start | bytes 786436
  60.4 22.3 %copy-start.6 = (pred[512,512]{0,1:T(8,128)(4,1)S(1)}, pred[512,512]{0,1:T(8,128)(4,1)}, u32[]{:S(2)}) copy-start(pred[512,512]{0,1:T(8,128)(4,1)} %get-tuple-element.57) | copy-start | bytes 786436
  84.8 18.8 %copy-start.5 = (pred[512,512]{0,1:T(8,128)(4,1)S(1)}, pred[512,512]{0,1:T(8,128)(4,1)}, u32[]{:S(2)}) copy-start(pred[512,512]{0,1:T(8,128)(4,1)} %get-tuple-element.59) | copy-start | bytes 786436
  113.1 11.6 %copy-start.1 = (bf16[512,1024]{1,0:T(8,128)(2,1)S(1)}, bf16[512,1024]{1,0:T(8,128)(2,1)}, u32[]{:S(2)}) copy-start(bf16[512,1024]{1,0:T(8,128)(2,1)} %param.9) | copy-start | bytes 3145732
  129.0 6.5 %copy-start.10 = (bf16[27,1024]{1,0:T(8,128)(2,1)S(1)}, bf16[27,1024]{1,0:T(8,128)(2,1)}, u32[]{:S(2)}) copy-start(bf16[27,1024]{1,0:T(8,128)(2,1)} %param.17) | copy-start | bytes 165892
  130.9 10.6 %collective-permute-start.5 = (bf16[1,8,16,1024]{3,2,1,0:T(8,128)(2,1)S(1)}, bf16[1,8,16,1024]{3,2,1,0:T(8,128)(2,1)S(1)}, u32[]{:S(2)}, u32[]{:S(2)}) collective-permute-start(bf16[1,8,16,1024]{3,2,1,0:T(8,128)(2,1)S(1)} %bitcast.107), channel_id=1, source_target_pairs={{2,0},{4,2},{6,4},{8,6},{10,8},{12,10},{14,12},{0,14},{3,1},{5,3},... | collective-permute-start | bytes 786440 | tf_op jit(solution)/shard_map/ppermute | solution.py:33
  135.5 10.9 %collective-permute-start.4 = (bf16[1,8,16,1024]{3,2,1,0:T(8,128)(2,1)S(1)}, bf16[1,8,16,1024]{3,2,1,0:T(8,128)(2,1)S(1)}, u32[]{:S(2)}, u32[]{:S(2)}) collective-permute-start(bf16[1,8,16,1024]{3,2,1,0:T(8,128)(2,1)S(1)} %bitcast.106), channel_id=1, source_target_pairs={{0,2},{2,4},{4,6},{6,8},{8,10},{10,12},{12,14},{14,0},{1,3},{3,5},... | collective-permute-start | bytes 786440 | tf_op jit(solution)/shard_map/ppermute | solution.py:32
  147.5 7.9 %copy-start.2 = (bf16[512,1024]{1,0:T(8,128)(2,1)S(1)}, bf16[512,1024]{1,0:T(8,128)(2,1)}, u32[]{:S(2)}) copy-start(bf16[512,1024]{1,0:T(8,128)(2,1)} %reduce-scatter.2.cloned.1.call-done) | copy-start | bytes 3145732
  (1 other events, 1.3 us)
Sparse Core Ops, SparseCore 0:
  8.9 13.2 all-gather.1
  113.2 11.4 reduce-scatter.1
where the time goes:
time: 165 us; the launch traced here: 164 us
  waiting for transfers between devices  81.4 us (49%)
  other arithmetic  23.4 us (14%)
  matrix products  19.5 us (12%)
  between operations  13.8 us (8%)
  starting transfers between devices  12.9 us (8%)
  local copies, waits for them, and re-layouts  10.9 us (7%)
  blocking collectives  2.47 us (1%)
    ppermute x4, waiting for transfers between devices, passed_along(): return lax.ppermute(value, axis, pairs)  46.5 us
    all_gather x1, waiting for transfers between devices, on_device(): full_rows = lax.all_gather(tokens, 'mp', axis=1, tiled=True)  11.9 us
    reduce_scatter x1, waiting for transfers between devices, on_device(): lax.psum_scatter(partial_value.astype(jnp.bfloat16), 'mp', scatter_dimens...  11.5 us
    ppermute x4, starting transfers between devices, passed_along(): return lax.ppermute(value, axis, pairs)  8.32 us
    add x1, other arithmetic, on_device(): conv_sum = conv_sum + window * conv_taps[(dz_off * 3 + dy_off) * 3 + dx_off]  7.9 us
    dot_general x5, matrix products, attend(): jnp.einsum('qhd,khd->hqk', queries, key_blk, preferred_element_type=jnp.f...  6.84 us
    ppermute x1, waiting for transfers between devices, with_halo(): after = lax.ppermute(initial, axis, down)  5.91 us
    slice x4, local copies, waits for them, and re-layouts, attend(): key_blk = kv_block[0].reshape(tok_rows, heads_here, HD)  5.11 us
  transfers between devices with their start and end apart: 8, of which 7 were waited for; matrix products, arithmetic and copies ran while one was open for 15% of the time, Pallas kernels for 0%

commit v1 on v0

v1 whole, which is shorter than its diff:
```python
import functools
import math

import jax
import jax.numpy as jnp
from jax import lax
from jax.experimental import pallas as pl
from jax.experimental.pallas import tpu as pltpu
from jax.sharding import PartitionSpec as P

HD = 128
GX = 16
PLANE = 128
RADIUS = 8
ZDEV = 4
EPS = 1e-06
MESH = pl.DeviceIdType.MESH
F32 = jnp.float32
BF16 = jnp.bfloat16

OWN, PAIR, BELOW, ABOVE, PASSED = range(5)


def block_kernel(
    n,
    x_ref,
    mod_ref,
    qg_ref,
    kg_ref,
    cw_ref,
    wq_hbm,
    wk_hbm,
    wv_hbm,
    wo_hbm,
    out_ref,
    wq,
    wk,
    wv,
    wo,
    x_other,
    normed,
    kv,
    qbuf,
    acc,
    den,
    attn,
    part_send,
    part_recv,
    part_own,
    stat_send,
    stat_recv,
    resid,
    pad,
    halo_send,
    halo_recv,
    taps,
    w_sem,
    x_sem,
    kv_send,
    kv_recv,
    part_sem,
    stat_sem,
    halo_ss,
    halo_rs,
):
    toks, half = x_ref.shape
    width = 2 * half
    heads = qbuf.shape[0]
    b = lax.axis_index("batch")
    s = lax.axis_index("seq")
    m = lax.axis_index("mp")
    odd = lax.rem(s, 2)
    pair = s + 1 - 2 * odd
    up1, down1 = lax.rem(s + 1, n), lax.rem(s + n - 1, n)
    up2, down2 = lax.rem(s + 2, n), lax.rem(s + n - 2, n)
    here = pl.multiple_of(m * half, half)
    there = pl.multiple_of((1 - m) * half, half)

    loads = []
    for i, (src, dst) in enumerate(((wk_hbm, wk), (wv_hbm, wv), (wq_hbm, wq), (wo_hbm, wo))):
        load = pltpu.make_async_copy(src, dst, w_sem.at[i])
        load.start()
        loads.append(load)

    peers = [(b, s, 1 - m), (b, up1, m), (b, down1, m), (b, up2, m), (b, down2, m)]
    barrier = pltpu.get_barrier_semaphore()
    for peer in peers:
        pl.semaphore_signal(barrier, inc=1, device_id=peer, device_id_type=MESH)
    pl.semaphore_wait(barrier, len(peers))

    def to(peer, src, dst, send_sem, recv_sem):
        return pltpu.make_async_remote_copy(
            src_ref=src,
            dst_ref=dst,
            send_sem=send_sem,
            recv_sem=recv_sem,
            device_id=peer,
            device_id_type=MESH,
        )

    core = (b, s, 1 - m)
    x_copy = to(core, x_ref, x_other, x_sem.at[0], x_sem.at[1])
    x_copy.start()

    pad[:, 0:GX, :] = jnp.zeros((ZDEV + 2, GX, half), F32)
    pad[:, GX + PLANE :, :] = jnp.zeros((ZDEV + 2, GX, half), F32)
    taps[...] = cw_ref[...].astype(F32)
    acc[...] = jnp.zeros_like(acc)
    den[...] = jnp.zeros_like(den)
    x_copy.wait()

    rows_n = 64

    @pl.loop(0, toks // rows_n)
    def _(i):
        rows = pl.ds(pl.multiple_of(i * rows_n, rows_n), rows_n)
        mine = x_ref[rows, :].astype(F32)
        other = x_other[rows, :].astype(F32)
        total = jnp.sum(mine, axis=-1, keepdims=True) + jnp.sum(other, axis=-1, keepdims=True)
        square = jnp.sum(mine * mine, axis=-1, keepdims=True) + jnp.sum(
            other * other, axis=-1, keepdims=True
        )
        mean = total / width
        inv = lax.rsqrt(square / width - mean * mean + EPS)
        for vals, cols in ((mine, pl.ds(here, half)), (other, pl.ds(there, half))):
            normed[rows, cols] = (
                (vals - mean) * inv * (1.0 + mod_ref[1:2, cols]) + mod_ref[0:1, cols]
            ).astype(BF16)

    fwd_slot = ABOVE - odd
    back_slot = BELOW + odd
    fwd_dst = lax.rem(s + n - 2 + 4 * odd, n)
    back_dst = lax.rem(s + 2 + n - 4 * odd, n)

    def send_fwd(h):
        return to((b, fwd_dst, m), kv.at[OWN, h], kv.at[fwd_slot, h], kv_send.at[0, h], kv_recv.at[0, h])

    def send_pair(h):
        return to((b, pair, m), kv.at[OWN, h], kv.at[PAIR, h], kv_send.at[1, h], kv_recv.at[1, h])

    def send_back(h):
        return to((b, back_dst, m), kv.at[OWN, h], kv.at[back_slot, h], kv_send.at[2, h], kv_recv.at[2, h])

    def send_on(h):
        return to((b, pair, m), kv.at[fwd_slot, h], kv.at[PASSED, h], kv_send.at[3, h], kv_recv.at[3, h])

    def head_norm(vals, gain):
        mean_sq = jnp.mean(vals * vals, axis=-1, keepdims=True)
        return vals * lax.rsqrt(mean_sq + EPS) * gain

    loads[0].wait()
    loads[1].wait()

    @pl.loop(0, heads // 2)
    def _(j):
        cols = pl.ds(pl.multiple_of(j * 2 * HD, 2 * HD), 2 * HD)
        keys = jnp.dot(normed[...], wk[:, cols], preferred_element_type=F32)
        for e in range(2):
            kv[OWN, 2 * j + e, :, 0:HD] = head_norm(
                keys[:, e * HD : (e + 1) * HD], kg_ref[...]
            ).astype(BF16)
        values = jnp.dot(normed[...], wv[:, cols], preferred_element_type=F32)
        for e in range(2):
            kv[OWN, 2 * j + e, :, HD:] = values[:, e * HD : (e + 1) * HD].astype(BF16)
        for e in range(2):
            send_fwd(2 * j + e).start()
            send_pair(2 * j + e).start()

    @pl.loop(0, heads)
    def _(h):
        send_back(h).start()

    loads[2].wait()

    @pl.loop(0, heads // 2)
    def _(j):
        cols = pl.ds(pl.multiple_of(j * 2 * HD, 2 * HD), 2 * HD)
        queries = jnp.dot(normed[...], wq[:, cols], preferred_element_type=F32)
        for e in range(2):
            qbuf[2 * j + e] = (
                head_norm(queries[:, e * HD : (e + 1) * HD], qg_ref[...]) * HD ** (-0.5)
            ).astype(BF16)

    rows_q = 256

    def attend(slot, h, sign):
        keys = kv[slot, h, :, 0:HD]
        values = kv[slot, h, :, HD:]
        for r in range(toks // rows_q):
            rows = pl.ds(r * rows_q, rows_q)
            scores = lax.dot_general(
                qbuf[h, rows, :], keys, (((1,), (1,)), ((), ())), preferred_element_type=F32
            )
            weights = jnp.exp(scores)
            if sign is not None:
                q_plane = (lax.broadcasted_iota(jnp.int32, scores.shape, 0) + r * rows_q) // PLANE
                k_plane = lax.broadcasted_iota(jnp.int32, scores.shape, 1) // PLANE
                gap = 2 * ZDEV + (k_plane - q_plane) * sign
                weights = jnp.where(gap <= RADIUS, weights, 0.0)
            total = weights[:, 0:HD]
            for c in range(1, toks // HD):
                total = total + weights[:, c * HD : (c + 1) * HD]
            den[h, rows, :] += total
            acc[h, rows, :] += jnp.dot(weights.astype(BF16), values, preferred_element_type=F32)

    @pl.loop(0, heads)
    def _(h):
        attend(OWN, h, None)

    @pl.loop(0, heads)
    def _(h):
        send_fwd(h).wait_recv()
        send_on(h).start()
        send_pair(h).wait_recv()
        attend(PAIR, h, None)
        attend(fwd_slot, h, 1 - 2 * odd)

    @pl.loop(0, heads)
    def _(h):
        send_back(h).wait_recv()
        attend(back_slot, h, 2 * odd - 1)

    planes_of = ((0, ZDEV - 1), (1, 2))

    @pl.loop(0, heads)
    def _(h):
        send_on(h).wait_recv()
        attend(PASSED, h, None)
        cols = pl.ds(pl.multiple_of(h * HD, HD), HD)
        for p, planes in enumerate(planes_of):
            for e, plane in enumerate(planes):
                rows = pl.ds(plane * PLANE, PLANE)
                total = jnp.sum(den[h, rows, :], axis=-1, keepdims=True)
                attn[p, e * PLANE : (e + 1) * PLANE, cols] = (acc[h, rows, :] / total).astype(BF16)

    loads[3].wait()
    tile = 256

    def part_copy(p):
        return to(core, part_send.at[p], part_recv.at[p], part_sem.at[0, p], part_sem.at[1, p])

    def stat_copy(p):
        return to(core, stat_send.at[p], stat_recv.at[p], stat_sem.at[0, p], stat_sem.at[1, p])

    for p in range(2):

        @pl.loop(0, half // tile)
        def _(c):
            at = pl.multiple_of(c * tile, tile)
            src = pl.ds(pl.multiple_of(there + at, tile), tile)
            part_send[p, :, pl.ds(at, tile)] = jnp.dot(
                attn[p], wo[:, src], preferred_element_type=F32
            ).astype(BF16)

        part_copy(p).start()

    for p in range(2):

        @pl.loop(0, half // tile)
        def _(c):
            at = pl.multiple_of(c * tile, tile)
            src = pl.ds(pl.multiple_of(here + at, tile), tile)
            part_own[p, :, pl.ds(at, tile)] = jnp.dot(attn[p], wo[:, src], preferred_element_type=F32)

    mine = pl.ds(here, half)
    step = 32
    for p, planes in enumerate(planes_of):
        part_copy(p).wait_recv()
        for e, plane in enumerate(planes):

            @pl.loop(0, PLANE // step)
            def _(i):
                at = pl.multiple_of(i * step, step)
                local = pl.ds(pl.multiple_of(e * PLANE + at, step), step)
                attended = part_own[p, local, :] + part_recv[p, local, :].astype(F32)
                vals = (
                    x_ref[pl.ds(pl.multiple_of(plane * PLANE + at, step), step), :].astype(F32)
                    + mod_ref[2:3, mine] * attended
                )
                resid[plane, pl.ds(at, step), :] = vals
                lane = lax.broadcasted_iota(jnp.int32, (step, HD), 1)
                stat_send[p, local, :] = jnp.where(
                    lane < HD // 2,
                    jnp.sum(vals, axis=-1, keepdims=True),
                    jnp.sum(vals * vals, axis=-1, keepdims=True),
                )

        stat_copy(p).start()

    def halo_up():
        return to((b, up1, m), halo_send.at[1], halo_recv.at[0], halo_ss.at[0], halo_rs.at[0])

    def halo_down():
        return to((b, down1, m), halo_send.at[0], halo_recv.at[1], halo_ss.at[1], halo_rs.at[1])

    for p, planes in enumerate(planes_of):
        stat_copy(p).wait_recv()
        for e, plane in enumerate(planes):

            @pl.loop(0, PLANE // step)
            def _(i):
                at = pl.multiple_of(i * step, step)
                local = pl.ds(pl.multiple_of(e * PLANE + at, step), step)
                stats = stat_send[p, local, :] + stat_recv[p, local, :]
                center = stats[:, 0:1] / width
                spread = stats[:, HD // 2 : HD // 2 + 1] / width - center * center
                shaped = (
                    (resid[plane, pl.ds(at, step), :] - center)
                    * lax.rsqrt(spread + EPS)
                    * (1.0 + mod_ref[4:5, mine])
                    + mod_ref[3:4, mine]
                ).astype(BF16)
                pad[plane + 1, pl.ds(pl.multiple_of(GX + at, GX), step), :] = shaped.astype(F32)
                if p == 0:
                    halo_send[e, pl.ds(at, step), :] = shaped

        if p == 0:
            halo_up().start()
            halo_down().start()

    rows_c = 64

    def convolve(plane, lc):
        lane_at = pl.multiple_of(lc * HD, HD)
        lanes = pl.ds(lane_at, HD)
        gate = mod_ref[5:6, pl.ds(pl.multiple_of(here + lane_at, HD), HD)]
        col = lax.rem(lax.broadcasted_iota(jnp.int32, (rows_c, HD), 0), GX)
        for r in range(PLANE // rows_c):
            sums = [None] * 3
            for dz in range(3):
                for dy in range(3):
                    window = pad[plane + dz, pl.ds(r * rows_c + GX * dy, rows_c), lanes]
                    for dx in range(3):
                        k = (dz * 3 + dy) * 3 + dx
                        term = window * taps[k : k + 1, lanes]
                        sums[dx] = term if sums[dx] is None else sums[dx] + term
            v = (
                sums[1]
                + jnp.where(col > 0, pltpu.roll(sums[0], 1, 0), 0.0)
                + jnp.where(col < GX - 1, pltpu.roll(sums[2], rows_c - 1, 0), 0.0)
            )
            gelu = 0.5 * v * (1.0 + jnp.tanh(math.sqrt(2.0 / math.pi) * (v + 0.044715 * (v * v * v))))
            result = resid[plane, pl.ds(r * rows_c, rows_c), lanes] + gate * gelu
            at = pl.multiple_of(plane * PLANE + r * rows_c, rows_c)
            out_ref[pl.ds(at, rows_c), lanes] = result.astype(BF16)

    chunks = half // HD

    @pl.loop(0, 2 * chunks)
    def _(i):
        convolve(1 + i // chunks, i % chunks)

    halo_up().wait_recv()
    halo_down().wait_recv()

    @pl.loop(0, PLANE // step)
    def _(i):
        at = pl.multiple_of(i * step, step)
        for e, plane in enumerate((0, ZDEV + 1)):
            pad[plane, pl.ds(pl.multiple_of(GX + at, GX), step), :] = halo_recv[
                e, pl.ds(at, step), :
            ].astype(F32)

    @pl.loop(0, 2 * chunks)
    def _(i):
        convolve((ZDEV - 1) * (i // chunks), i % chunks)

    @pl.loop(0, heads)
    def _(h):
        send_fwd(h).wait_send()
        send_pair(h).wait_send()
        send_back(h).wait_send()
        send_on(h).wait_send()

    for p in range(2):
        part_copy(p).wait_send()
        stat_copy(p).wait_send()
    halo_up().wait_send()
    halo_down().wait_send()


def on_device(n, tokens, modulation, query_weight, key_weight, value_weight, out_weight, query_gain, key_gain, conv_weight):
    toks, half = tokens.shape
    inner = query_weight.shape[1]
    heads = inner // HD
    vmem = pl.BlockSpec(memory_space=pltpu.VMEM)
    hbm = pl.BlockSpec(memory_space=pl.ANY)
    dma = pltpu.SemaphoreType.DMA
    return pl.pallas_call(
        functools.partial(block_kernel, n),
        out_shape=jax.ShapeDtypeStruct((toks, half), BF16),
        in_specs=[vmem] * 5 + [hbm] * 4,
        out_specs=vmem,
        scratch_shapes=[
            pltpu.VMEM(query_weight.shape, BF16),
            pltpu.VMEM(key_weight.shape, BF16),
            pltpu.VMEM(value_weight.shape, BF16),
            pltpu.VMEM(out_weight.shape, BF16),
            pltpu.VMEM((toks, half), BF16),
            pltpu.VMEM((toks, 2 * half), BF16),
            pltpu.VMEM((5, heads, toks, 2 * HD), BF16),
            pltpu.VMEM((heads, toks, HD), BF16),
            pltpu.VMEM((heads, toks, HD), F32),
            pltpu.VMEM((heads, toks, HD), F32),
            pltpu.VMEM((2, toks // 2, inner), BF16),
            pltpu.VMEM((2, toks // 2, half), BF16),
            pltpu.VMEM((2, toks // 2, half), BF16),
            pltpu.VMEM((2, toks // 2, half), F32),
            pltpu.VMEM((2, toks // 2, HD), F32),
            pltpu.VMEM((2, toks // 2, HD), F32),
            pltpu.VMEM((ZDEV, PLANE, half), F32),
            pltpu.VMEM((ZDEV + 2, PLANE + 2 * GX, half), F32),
            pltpu.VMEM((2, PLANE, half), BF16),
            pltpu.VMEM((2, PLANE, half), BF16),
            pltpu.VMEM((27, half), F32),
            dma((4,)),
            dma((2,)),
            dma((4, heads)),
            dma((4, heads)),
            dma((2, 2)),
            dma((2, 2)),
            dma((2,)),
            dma((2,)),
        ],
        compiler_params=pltpu.CompilerParams(
            collective_id=0, has_side_effects=True, vmem_limit_bytes=52 << 20
        ),
    )(
        tokens,
        modulation,
        query_gain.reshape(1, HD),
        key_gain.reshape(1, HD),
        conv_weight,
        query_weight,
        key_weight,
        value_weight,
        out_weight,
    )


def solution(mesh):
    return jax.shard_map(
        functools.partial(on_device, mesh.shape["seq"]),
        mesh=mesh,
        in_specs=(
            P(("batch", "seq"), "mp"),
            P("batch", None),
            P(None, "mp"),
            P(None, "mp"),
            P(None, "mp"),
            P("mp", None),
            P(),
            P(),
            P(None, "mp"),
        ),
        out_specs=P(("batch", "seq"), "mp"),
        check_vma=False,
    )
```

time: 165 us -> 90.2 us (0.55)
  Pallas kernels: 0 us -> 86 us
  waiting for transfers between devices: 81.4 us -> 0 us
  other arithmetic: 23.4 us -> 0 us
  matrix products: 19.5 us -> 0 us
  between operations: 13.8 us -> 0.01 us
  starting transfers between devices: 12.9 us -> 0 us
  local copies, waits for them, and re-layouts: 10.9 us -> 3.96 us
  blocking collectives: 2.47 us -> 0 us
    pallas_call x0 -> x1, Pallas kernels: none -> 86 us  [on_device(): pl.pallas_call(functools.partial(block_kernel, n), out_shape=jax.ShapeDty...]
    ppermute x6 -> x0, waiting for transfers between devices: 57.3 us -> none  [the longest x4 46.5 us: passed_along(): return lax.ppermute(value, axis, pairs)]
    dot_general x14 -> x0, matrix products: 19.5 us -> none  [the longest x5 6.84 us: attend(): jnp.einsum('qhd,khd->hqk', queries, key_blk, preferred_element_type=jnp.f...]
    ppermute x6 -> x0, starting transfers between devices: 12.9 us -> none  [the longest x4 8.32 us: passed_along(): return lax.ppermute(value, axis, pairs)]
    all_gather x1 -> x0, waiting for transfers between devices: 11.9 us -> none  [on_device(): full_rows = lax.all_gather(tokens, 'mp', axis=1, tiled=True)]
    reduce_scatter x1 -> x0, waiting for transfers between devices: 11.5 us -> none  [on_device(): lax.psum_scatter(partial_value.astype(jnp.bfloat16), 'mp', scatter_dimens...]
    add x5 -> x0, other arithmetic: 7.93 us -> none  [the longest x1 7.9 us: on_device(): conv_sum = conv_sum + window * conv_taps[(dz_off * 3 + dy_off) * 3 + dx_off]]
    convert_element_type x5 -> x0, other arithmetic: 6.51 us -> none  [the longest x1 2.07 us: on_device(): return mixed.astype(jnp.bfloat16)]
  transfers between devices with their start and end apart: 8 -> 0, of which waited for: 7 -> 0; matrix products, arithmetic and copies ran while one was open for 15% -> 0% of each run, Pallas kernels for 0% -> 0%
where the time goes in v1:
time: 90.2 us; the launch traced here: 90 us
  Pallas kernels  86 us (95%)
  local copies, waits for them, and re-layouts  3.96 us (4%)
    pallas_call x1, Pallas kernels, on_device(): pl.pallas_call(functools.partial(block_kernel, n), out_shape=jax.ShapeDty...  86 us
    unnamed x9, local copies, waits for them, and re-layouts  3.96 us

profile of v1, /device:TPU:0, one launch (start us, length us, event | category | flops | bytes accessed | tf_op | source)
XLA Modules:
  0.0 90.0 jit_solution(3962609786941764944)
XLA Ops:
  0.0 0.0 copy-start
  0.0 0.8 copy-done
  0.8 0.0 copy-start.1
  0.8 0.8 copy-done.1
  1.7 0.0 copy-start.2
  1.7 0.7 copy-done.2
  2.3 0.0 copy-start.3
  2.3 0.7 copy-done.3
  3.0 86.0 %shard_map.91 = bf16[512,1024]{1,0:T(8,128)(2,1)S(1)} custom-call(bf16[512,1024]{1,0:T(8,128)(2,1)} %x_ref.1, f32[6,2048]{1,0:T(8,128)S(1)} %copy-done, f32[1,128]{1,0:T(1,128)S(1)} %bitcast.2, f32[1,128]{1,0:T(1,128)S(1)} %bitcast.3, bf16[27,1024]{1,0:T(8,128)(2,1)S(1)} %copy-done.1, bf16[2048,512]{1,0:T(8,128)(2,1)} %wq_hbm.1, bf16[2048,512]{1,0:T(8,128)(2,1)} %wk_hbm.1, ...), custom_call_target="tpu_custom_call" | custom-call | tf_op jit(solution)/shard_map/pallas_call | solution.py:389
  89.0 1.0 %copy.11 = bf16[512,1024]{1,0:T(8,128)(2,1)} copy(bf16[512,1024]{1,0:T(8,128)(2,1)S(1)} %shard_map.91) | data formatting | bytes 2097152
Async XLA Ops:
  0.0 0.8 copy-start
  0.8 0.8 copy-start.1
  1.7 0.7 copy-start.2
  2.3 0.7 copy-start.3

commit v2 on v1

--- a/solution.py
+++ b/solution.py
@@ -24,20 +24,26 @@
 def block_kernel(
     n,
     x_ref,
-    mod_ref,
-    qg_ref,
-    kg_ref,
-    cw_ref,
+    mod_hbm,
+    qg_hbm,
+    kg_hbm,
+    cw_hbm,
     wq_hbm,
     wk_hbm,
     wv_hbm,
     wo_hbm,
     out_ref,
+    mod_ref,
+    qg_ref,
+    kg_ref,
+    cw_ref,
     wq,
     wk,
     wv,
     wo,
     x_other,
+    x_in,
+    x_in_other,
     normed,
     kv,
     qbuf,
@@ -51,13 +57,15 @@
     stat_recv,
     resid,
     pad,
-    halo_send,
-    halo_recv,
     taps,
     w_sem,
     x_sem,
     kv_send,
     kv_recv,
+    xi_send,
+    xi_recv,
+    xo_send,
+    xo_recv,
     part_sem,
     stat_sem,
     halo_ss,
@@ -77,7 +85,9 @@
     there = pl.multiple_of((1 - m) * half, half)
 
     loads = []
-    for i, (src, dst) in enumerate(((wk_hbm, wk), (wv_hbm, wv), (wq_hbm, wq), (wo_hbm, wo))):
+    sources = (wk_hbm, wv_hbm, wq_hbm, wo_hbm, mod_hbm, qg_hbm, kg_hbm, cw_hbm)
+    targets = (wk, wv, wq, wo, mod_ref, qg_ref, kg_ref, cw_ref)
+    for i, (src, dst) in enumerate(zip(sources, targets)):
         load = pltpu.make_async_copy(src, dst, w_sem.at[i])
         load.start()
         loads.append(load)
@@ -102,6 +112,52 @@
     x_copy = to(core, x_ref, x_other, x_sem.at[0], x_sem.at[1])
     x_copy.start()
 
+    late = pl.ds(PLANE, (ZDEV - 2) * PLANE)
+
+    fwd_slot = ABOVE - odd
+    back_slot = BELOW + odd
+    fwd_dst = lax.rem(s + n - 2 + 4 * odd, n)
+    back_dst = lax.rem(s + 2 + n - 4 * odd, n)
+
+    def send_fwd(h):
+        return to((b, fwd_dst, m), kv.at[OWN, h, late], kv.at[fwd_slot, h, late], kv_send.at[0, h], kv_recv.at[0, h])
+
+    def send_pair(h):
+        return to((b, pair, m), kv.at[OWN, h, late], kv.at[PAIR, h, late], kv_send.at[1, h], kv_recv.at[1, h])
+
+    def send_back(h):
+        return to((b, back_dst, m), kv.at[OWN, h, late], kv.at[back_slot, h, late], kv_send.at[2, h], kv_recv.at[2, h])
+
+    def send_on(h):
+        return to((b, pair, m), kv.at[fwd_slot, h, late], kv.at[PASSED, h, late], kv_send.at[3, h], kv_recv.at[3, h])
+
+    def early(e):
+        return pl.ds(e * (ZDEV - 1) * PLANE, PLANE)
+
+    def x_to(k, dst, src, slot, e):
+        return to((b, dst, m), src, x_in.at[slot - 1, e], xi_send.at[k, e], xi_recv.at[k, e])
+
+    def x_fwd(e):
+        return x_to(0, fwd_dst, x_ref.at[early(e)], fwd_slot, e)
+
+    def x_pair(e):
+        return x_to(1, pair, x_ref.at[early(e)], PAIR, e)
+
+    def x_back(e):
+        return x_to(2, back_dst, x_ref.at[early(e)], back_slot, e)
+
+    def x_on(e):
+        return x_to(3, pair, x_in.at[fwd_slot - 1, e], PASSED, e)
+
+    def x_core(k, slot, e):
+        return to(core, x_in.at[slot - 1, e], x_in_other.at[slot - 1, e], xo_send.at[k, e], xo_recv.at[k, e])
+
+    for send in (x_fwd, x_pair, x_back):
+        for e in range(2):
+            send(e).start()
+
+    for load in loads[4:]:
+        load.wait()
     pad[:, 0:GX, :] = jnp.zeros((ZDEV + 2, GX, half), F32)
     pad[:, GX + PLANE :, :] = jnp.zeros((ZDEV + 2, GX, half), F32)
     taps[...] = cw_ref[...].astype(F32)
@@ -111,11 +167,9 @@
 
     rows_n = 64
 
-    @pl.loop(0, toks // rows_n)
-    def _(i):
-        rows = pl.ds(pl.multiple_of(i * rows_n, rows_n), rows_n)
-        mine = x_ref[rows, :].astype(F32)
-        other = x_other[rows, :].astype(F32)
+    def norm_rows(mine_bf, other_bf, rows):
+        mine = mine_bf.astype(F32)
+        other = other_bf.astype(F32)
         total = jnp.sum(mine, axis=-1, keepdims=True) + jnp.sum(other, axis=-1, keepdims=True)
         square = jnp.sum(mine * mine, axis=-1, keepdims=True) + jnp.sum(
             other * other, axis=-1, keepdims=True
@@ -127,22 +181,10 @@
                 (vals - mean) * inv * (1.0 + mod_ref[1:2, cols]) + mod_ref[0:1, cols]
             ).astype(BF16)
 
-    fwd_slot = ABOVE - odd
-    back_slot = BELOW + odd
-    fwd_dst = lax.rem(s + n - 2 + 4 * odd, n)
-    back_dst = lax.rem(s + 2 + n - 4 * odd, n)
-
-    def send_fwd(h):
-        return to((b, fwd_dst, m), kv.at[OWN, h], kv.at[fwd_slot, h], kv_send.at[0, h], kv_recv.at[0, h])
-
-    def send_pair(h):
-        return to((b, pair, m), kv.at[OWN, h], kv.at[PAIR, h], kv_send.at[1, h], kv_recv.at[1, h])
-
-    def send_back(h):
-        return to((b, back_dst, m), kv.at[OWN, h], kv.at[back_slot, h], kv_send.at[2, h], kv_recv.at[2, h])
-
-    def send_on(h):
-        return to((b, pair, m), kv.at[fwd_slot, h], kv.at[PASSED, h], kv_send.at[3, h], kv_recv.at[3, h])
+    @pl.loop(0, toks // rows_n)
+    def _(i):
+        rows = pl.ds(pl.multiple_of(i * rows_n, rows_n), rows_n)
+        norm_rows(x_ref[rows, :], x_other[rows, :], rows)
 
     def head_norm(vals, gain):
         mean_sq = jnp.mean(vals * vals, axis=-1, keepdims=True)
@@ -169,6 +211,13 @@
     @pl.loop(0, heads)
     def _(h):
         send_back(h).start()
+
+    for e in range(2):
+        x_fwd(e).wait_recv()
+        x_on(e).start()
+        x_core(0, fwd_slot, e).start()
+        x_pair(e).wait_recv()
+        x_core(1, PAIR, e).start()
 
     loads[2].wait()
 
@@ -207,6 +256,43 @@
     def _(h):
         attend(OWN, h, None)
 
+    def project(k, slot):
+        for e in range(2):
+            x_core(k, slot, e).wait_recv()
+
+            @pl.loop(0, PLANE // rows_n)
+            def _(i):
+                rows = pl.ds(pl.multiple_of(i * rows_n, rows_n), rows_n)
+                norm_rows(
+                    x_in[slot - 1, e, rows, :],
+                    x_in_other[slot - 1, e, rows, :],
+                    pl.ds(pl.multiple_of(e * PLANE + i * rows_n, rows_n), rows_n),
+                )
+
+        @pl.loop(0, heads // 2)
+        def _(j):
+            cols = pl.ds(pl.multiple_of(j * 2 * HD, 2 * HD), 2 * HD)
+            keys = jnp.dot(normed[0 : 2 * PLANE, :], wk[:, cols], preferred_element_type=F32)
+            values = jnp.dot(normed[0 : 2 * PLANE, :], wv[:, cols], preferred_element_type=F32)
+            for d in range(2):
+                key_d = head_norm(keys[:, d * HD : (d + 1) * HD], kg_ref[...]).astype(BF16)
+                value_d = values[:, d * HD : (d + 1) * HD].astype(BF16)
+                for e in range(2):
+                    part = slice(e * PLANE, (e + 1) * PLANE)
+                    kv[slot, 2 * j + d, early(e), 0:HD] = key_d[part]
+                    kv[slot, 2 * j + d, early(e), HD:] = value_d[part]
+
+    project(0, fwd_slot)
+    project(1, PAIR)
+    for e in range(2):
+        x_back(e).wait_recv()
+        x_core(2, back_slot, e).start()
+    project(2, back_slot)
+    for e in range(2):
+        x_on(e).wait_recv()
+        x_core(3, PASSED, e).start()
+    project(3, PASSED)
+
     @pl.loop(0, heads)
     def _(h):
         send_fwd(h).wait_recv()
@@ -242,8 +328,30 @@
     def stat_copy(p):
         return to(core, stat_send.at[p], stat_recv.at[p], stat_sem.at[0, p], stat_sem.at[1, p])
 
-    for p in range(2):
-
+    def halo_up():
+        return to(
+            (b, up1, m),
+            attn.at[0, pl.ds(PLANE, PLANE)],
+            attn.at[2, pl.ds(0, PLANE)],
+            halo_ss.at[0],
+            halo_rs.at[0],
+        )
+
+    def halo_down():
+        return to(
+            (b, down1, m),
+            attn.at[0, pl.ds(0, PLANE)],
+            attn.at[2, pl.ds(PLANE, PLANE)],
+            halo_ss.at[1],
+            halo_rs.at[1],
+        )
+
+    halo_up().start()
+    halo_down().start()
+    mine = pl.ds(here, half)
+    step = 32
+
+    def part(p):
         @pl.loop(0, half // tile)
         def _(c):
             at = pl.multiple_of(c * tile, tile)
@@ -254,29 +362,31 @@
 
         part_copy(p).start()
 
-    for p in range(2):
-
+    def own(p):
         @pl.loop(0, half // tile)
         def _(c):
             at = pl.multiple_of(c * tile, tile)
             src = pl.ds(pl.multiple_of(here + at, tile), tile)
             part_own[p, :, pl.ds(at, tile)] = jnp.dot(attn[p], wo[:, src], preferred_element_type=F32)
 
-    mine = pl.ds(here, half)
-    step = 32
-    for p, planes in enumerate(planes_of):
+    halo_slots = (3 - 3 * odd, 3 * odd)
+
+    def residual(p):
         part_copy(p).wait_recv()
-        for e, plane in enumerate(planes):
+        for e in range(2):
 
             @pl.loop(0, PLANE // step)
             def _(i):
                 at = pl.multiple_of(i * step, step)
                 local = pl.ds(pl.multiple_of(e * PLANE + at, step), step)
                 attended = part_own[p, local, :] + part_recv[p, local, :].astype(F32)
-                vals = (
-                    x_ref[pl.ds(pl.multiple_of(plane * PLANE + at, step), step), :].astype(F32)
-                    + mod_ref[2:3, mine] * attended
-                )
+                if p < 2:
+                    plane = planes_of[p][e]
+                    base = x_ref[pl.ds(pl.multiple_of(plane * PLANE + at, step), step), :]
+                else:
+                    plane = ZDEV + e
+                    base = x_in[halo_slots[e], 1 - e, pl.ds(at, step), :]
+                vals = base.astype(F32) + mod_ref[2:3, mine] * attended
                 resid[plane, pl.ds(at, step), :] = vals
                 lane = lax.broadcasted_iota(jnp.int32, (step, HD), 1)
                 stat_send[p, local, :] = jnp.where(
@@ -287,15 +397,9 @@
 
         stat_copy(p).start()
 
-    def halo_up():
-        return to((b, up1, m), halo_send.at[1], halo_recv.at[0], halo_ss.at[0], halo_rs.at[0])
-
-    def halo_down():
-        return to((b, down1, m), halo_send.at[0], halo_recv.at[1], halo_ss.at[1], halo_rs.at[1])
-
-    for p, planes in enumerate(planes_of):
+    def shape(p):
         stat_copy(p).wait_recv()
-        for e, plane in enumerate(planes):
+        for e in range(2):
 
             @pl.loop(0, PLANE // step)
             def _(i):
@@ -304,19 +408,29 @@
                 stats = stat_send[p, local, :] + stat_recv[p, local, :]
                 center = stats[:, 0:1] / width
                 spread = stats[:, HD // 2 : HD // 2 + 1] / width - center * center
+                plane = planes_of[p][e] if p < 2 else ZDEV + e
+                slab = plane + 1 if p < 2 else e * (ZDEV + 1)
                 shaped = (
                     (resid[plane, pl.ds(at, step), :] - center)
                     * lax.rsqrt(spread + EPS)
                     * (1.0 + mod_ref[4:5, mine])
                     + mod_ref[3:4, mine]
                 ).astype(BF16)
-                pad[plane + 1, pl.ds(pl.multiple_of(GX + at, GX), step), :] = shaped.astype(F32)
-                if p == 0:
-                    halo_send[e, pl.ds(at, step), :] = shaped
-
-        if p == 0:
-            halo_up().start()
-            halo_down().start()
+                pad[slab, pl.ds(pl.multiple_of(GX + at, GX), step), :] = shaped.astype(F32)
+
+    part(0)
+    part(1)
+    own(0)
+    own(1)
+    residual(0)
+    residual(1)
+    halo_up().wait_recv()
+    halo_down().wait_recv()
+    part(2)
+    own(2)
+    shape(0)
+    shape(1)
+    residual(2)
 
     rows_c = 64
 
@@ -350,16 +464,7 @@
     def _(i):
         convolve(1 + i // chunks, i % chunks)
 
-    halo_up().wait_recv()
-    halo_down().wait_recv()
-
-    @pl.loop(0, PLANE // step)
-    def _(i):
-        at = pl.multiple_of(i * step, step)
-        for e, plane in enumerate((0, ZDEV + 1)):
-            pad[plane, pl.ds(pl.multiple_of(GX + at, GX), step), :] = halo_recv[
-                e, pl.ds(at, step), :
-            ].astype(F32)
+    shape(2)
 
     @pl.loop(0, 2 * chunks)
     def _(i):
@@ -372,7 +477,14 @@
         send_back(h).wait_send()
         send_on(h).wait_send()
 
-    for p in range(2):
+    for e in range(2):
+        x_fwd(e).wait_send()
+        x_pair(e).wait_send()
+        x_back(e).wait_send()
+        x_on(e).wait_send()
+        for k, slot in enumerate((fwd_slot, PAIR, back_slot, PASSED)):
+            x_core(k, slot, e).wait_send()
+    for p in range(3):
         part_copy(p).wait_send()
         stat_copy(p).wait_send()
     halo_up().wait_send()
@@ -384,46 +496,54 @@
     inner = query_weight.shape[1]
     heads = inner // HD
     vmem = pl.BlockSpec(memory_space=pltpu.VMEM)
-    hbm = pl.BlockSpec(memory_space=pl.ANY)
+    hbm = pl.BlockSpec(memory_space=pltpu.HBM)
     dma = pltpu.SemaphoreType.DMA
     return pl.pallas_call(
         functools.partial(block_kernel, n),
         out_shape=jax.ShapeDtypeStruct((toks, half), BF16),
-        in_specs=[vmem] * 5 + [hbm] * 4,
+        in_specs=[vmem] + [hbm] * 8,
         out_specs=vmem,
         scratch_shapes=[
+            pltpu.VMEM(modulation.shape, F32),
+            pltpu.VMEM((1, HD), F32),
+            pltpu.VMEM((1, HD), F32),
+            pltpu.VMEM(conv_weight.shape, BF16),
             pltpu.VMEM(query_weight.shape, BF16),
             pltpu.VMEM(key_weight.shape, BF16),
             pltpu.VMEM(value_weight.shape, BF16),
             pltpu.VMEM(out_weight.shape, BF16),
             pltpu.VMEM((toks, half), BF16),
+            pltpu.VMEM((4, 2, PLANE, half), BF16),
+            pltpu.VMEM((4, 2, PLANE, half), BF16),
             pltpu.VMEM((toks, 2 * half), BF16),
             pltpu.VMEM((5, heads, toks, 2 * HD), BF16),
             pltpu.VMEM((heads, toks, HD), BF16),
             pltpu.VMEM((heads, toks, HD), F32),
             pltpu.VMEM((heads, toks, HD), F32),
-            pltpu.VMEM((2, toks // 2, inner), BF16),
-            pltpu.VMEM((2, toks // 2, half), BF16),
-            pltpu.VMEM((2, toks // 2, half), BF16),
-            pltpu.VMEM((2, toks // 2, half), F32),
-            pltpu.VMEM((2, toks // 2, HD), F32),
-            pltpu.VMEM((2, toks // 2, HD), F32),
-            pltpu.VMEM((ZDEV, PLANE, half), F32),
+            pltpu.VMEM((3, 2 * PLANE, inner), BF16),
+            pltpu.VMEM((3, 2 * PLANE, half), BF16),
+            pltpu.VMEM((3, 2 * PLANE, half), BF16),
+            pltpu.VMEM((3, 2 * PLANE, half), F32),
+            pltpu.VMEM((3, 2 * PLANE, HD), F32),
+            pltpu.VMEM((3, 2 * PLANE, HD), F32),
+            pltpu.VMEM((ZDEV + 2, PLANE, half), F32),
             pltpu.VMEM((ZDEV + 2, PLANE + 2 * GX, half), F32),
-            pltpu.VMEM((2, PLANE, half), BF16),
-            pltpu.VMEM((2, PLANE, half), BF16),
             pltpu.VMEM((27, half), F32),
-            dma((4,)),
+            dma((8,)),
             dma((2,)),
             dma((4, heads)),
             dma((4, heads)),
-            dma((2, 2)),
-            dma((2, 2)),
+            dma((4, 2)),
+            dma((4, 2)),
+            dma((4, 2)),
+            dma((4, 2)),
+            dma((2, 3)),
+            dma((2, 3)),
             dma((2,)),
             dma((2,)),
         ],
         compiler_params=pltpu.CompilerParams(
-            collective_id=0, has_side_effects=True, vmem_limit_bytes=52 << 20
+            collective_id=0, has_side_effects=True, vmem_limit_bytes=60 << 20
         ),
     )(
         tokens,

time: 90.2 us -> 83.2 us (0.922)
  Pallas kernels: 86 us -> 80.8 us
  local copies, waits for them, and re-layouts: 3.96 us -> 2.26 us
    pallas_call x1, Pallas kernels: 86 us -> 80.8 us  [on_device(): pl.pallas_call(functools.partial(block_kernel, n), out_shape=jax.ShapeDty...]
    unnamed x9 -> x1, local copies, waits for them, and re-layouts: 3.96 us -> 2.26 us
where the time goes in v2:
time: 83.2 us; the launch traced here: 83.1 us
  Pallas kernels  80.8 us (97%)
  local copies, waits for them, and re-layouts  2.26 us (3%)
    pallas_call x1, Pallas kernels, on_device(): pl.pallas_call(functools.partial(block_kernel, n), out_shape=jax.ShapeDty...  80.8 us
    unnamed x1, local copies, waits for them, and re-layouts  2.26 us

profile of v2, /device:TPU:0, one launch (start us, length us, event | category | flops | bytes accessed | tf_op | source)
XLA Modules:
  0.0 83.1 jit_solution(7584076211850790712)
XLA Ops:
  0.0 80.8 %shard_map.91 = bf16[512,1024]{1,0:T(8,128)(2,1)} custom-call(bf16[512,1024]{1,0:T(8,128)(2,1)} %x_ref.1, f32[6,2048]{1,0:T(8,128)} %mod_hbm.1, f32[1,128]{1,0:T(1,128)} %bitcast.2, f32[1,128]{1,0:T(1,128)} %bitcast.3, bf16[27,1024]{1,0:T(8,128)(2,1)} %cw_hbm.1, bf16[2048,512]{1,0:T(8,128)(2,1)} %wq_hbm.1, bf16[2048,512]{1,0:T(8,128)(2,1)} %wk_hbm.1, ...), custom_call_target="tpu_custom_call" | custom-call | tf_op jit(solution)/shard_map/pallas_call | solution.py:501
  80.8 2.3 %copy.11 = bf16[512,1024]{1,0:T(8,128)(2,1)} copy(bf16[512,1024]{1,0:T(8,128)(2,1)} %shard_map.91) | data formatting | bytes 2097152

commit v3 on v2

--- a/solution.py
+++ b/solution.py
@@ -306,6 +306,27 @@
         send_back(h).wait_recv()
         attend(back_slot, h, 2 * odd - 1)
 
+    def head_cols(h):
+        return pl.ds(pl.multiple_of(h * HD, HD), HD)
+
+    def halo_up(h):
+        return to(
+            (b, up1, m),
+            attn.at[0, pl.ds(PLANE, PLANE), head_cols(h)],
+            attn.at[2, pl.ds(0, PLANE), head_cols(h)],
+            halo_ss.at[0, h],
+            halo_rs.at[0, h],
+        )
+
+    def halo_down(h):
+        return to(
+            (b, down1, m),
+            attn.at[0, pl.ds(0, PLANE), head_cols(h)],
+            attn.at[2, pl.ds(PLANE, PLANE), head_cols(h)],
+            halo_ss.at[1, h],
+            halo_rs.at[1, h],
+        )
+
     planes_of = ((0, ZDEV - 1), (1, 2))
 
     @pl.loop(0, heads)
@@ -318,6 +339,8 @@
                 rows = pl.ds(plane * PLANE, PLANE)
                 total = jnp.sum(den[h, rows, :], axis=-1, keepdims=True)
                 attn[p, e * PLANE : (e + 1) * PLANE, cols] = (acc[h, rows, :] / total).astype(BF16)
+        halo_up(h).start()
+        halo_down(h).start()
 
     loads[3].wait()
     tile = 256
@@ -328,26 +351,6 @@
     def stat_copy(p):
         return to(core, stat_send.at[p], stat_recv.at[p], stat_sem.at[0, p], stat_sem.at[1, p])
 
-    def halo_up():
-        return to(
-            (b, up1, m),
-            attn.at[0, pl.ds(PLANE, PLANE)],
-            attn.at[2, pl.ds(0, PLANE)],
-            halo_ss.at[0],
-            halo_rs.at[0],
-        )
-
-    def halo_down():
-        return to(
-            (b, down1, m),
-            attn.at[0, pl.ds(0, PLANE)],
-            attn.at[2, pl.ds(PLANE, PLANE)],
-            halo_ss.at[1],
-            halo_rs.at[1],
-        )
-
-    halo_up().start()
-    halo_down().start()
     mine = pl.ds(here, half)
     step = 32
 
@@ -424,8 +427,12 @@
     own(1)
     residual(0)
     residual(1)
-    halo_up().wait_recv()
-    halo_down().wait_recv()
+
+    @pl.loop(0, heads)
+    def _(h):
+        halo_up(h).wait_recv()
+        halo_down(h).wait_recv()
+
     part(2)
     own(2)
     shape(0)
@@ -487,8 +494,11 @@
     for p in range(3):
         part_copy(p).wait_send()
         stat_copy(p).wait_send()
-    halo_up().wait_send()
-    halo_down().wait_send()
+
+    @pl.loop(0, heads)
+    def _(h):
+        halo_up(h).wait_send()
+        halo_down(h).wait_send()
 
 
 def on_device(n, tokens, modulation, query_weight, key_weight, value_weight, out_weight, query_gain, key_gain, conv_weight):
@@ -539,8 +549,8 @@
             dma((4, 2)),
             dma((2, 3)),
             dma((2, 3)),
-            dma((2,)),
-            dma((2,)),
+            dma((2, heads)),
+            dma((2, heads)),
         ],
         compiler_params=pltpu.CompilerParams(
             collective_id=0, has_side_effects=True, vmem_limit_bytes=60 << 20

time: 83.2 us -> 84.3 us (1.013); the launches traced: 83.1 us -> 83.1 us
  no operation moved by 1% of the time
where the time goes in v3:
time: 84.3 us; the launch traced here: 83.1 us
  Pallas kernels  80.9 us (96%)
  local copies, waits for them, and re-layouts  2.26 us (3%)
    pallas_call x1, Pallas kernels, on_device(): pl.pallas_call(functools.partial(block_kernel, n), out_shape=jax.ShapeDty...  80.9 us
    unnamed x1, local copies, waits for them, and re-layouts  2.26 us

profile of v3, /device:TPU:0, one launch (start us, length us, event | category | flops | bytes accessed | tf_op | source)
XLA Modules:
  0.0 83.1 jit_solution(17542717750994670224)
XLA Ops:
  0.0 80.9 %shard_map.91 = bf16[512,1024]{1,0:T(8,128)(2,1)} custom-call(bf16[512,1024]{1,0:T(8,128)(2,1)} %x_ref.1, f32[6,2048]{1,0:T(8,128)} %mod_hbm.1, f32[1,128]{1,0:T(1,128)} %bitcast.2, f32[1,128]{1,0:T(1,128)} %bitcast.3, bf16[27,1024]{1,0:T(8,128)(2,1)} %cw_hbm.1, bf16[2048,512]{1,0:T(8,128)(2,1)} %wq_hbm.1, bf16[2048,512]{1,0:T(8,128)(2,1)} %wk_hbm.1, ...), custom_call_target="tpu_custom_call" | custom-call | tf_op jit(solution)/shard_map/pallas_call | solution.py:511
  80.9 2.3 %copy.11 = bf16[512,1024]{1,0:T(8,128)(2,1)} copy(bf16[512,1024]{1,0:T(8,128)(2,1)} %shard_map.91) | data formatting | bytes 2097152
